TPU v7x, 512 devices: a whole 4x4x16 slice. The times are simulated.
512 devices in a mesh: dp: 64 (over y, z), tensor: 8 (over x, core).
Axes of the slice: x: 4, y: 4, z: 16, core: 2. Of those that a mesh axis runs over, the one named last changes fastest.
Arguments:
- hidden: bfloat16 [16384, 8192], P('dp', 'tensor'), may hold values from -8 to 8
- norm_gain: float32 [8192], P('tensor'), may hold values from 0.5 to 1.5
- lm_head: bfloat16 [81920, 8192], P('dp', 'tensor'), may hold values from -8 to 8
- loss_count: int32 [64], P('dp'), may hold values from 0 to 6, as said below
- loss_pos: int32 [64, 6], P('dp'), may hold values from 0 to 255, as said below
- targets: int32 [64, 6], P('dp'), may hold values from 0 to 81919
- dest: int32 [64, 6], P('dp'), may hold values from -1 to 191, as said below
Outputs:
- hidden_grad: bfloat16 [16384, 8192], P('dp', 'tensor')
- row_loss: float32 [192], P('dp')
Inputs may be any that keep to these rules, and one draw needn't show every extreme that they name: `loss_count`: the counts sum to 192, and some dp index has 6 loss rows. `loss_pos`: in each row the first loss_count entries are distinct positions; later entries are ignored. `dest`: over all live slots every value from 0 to 191 appears exactly once, so each dp index receives exactly 3 rows (row p belongs to dp index p // 3); empty slots hold -1.
All inputs are finite; a program needn't handle non-finite values.
Results may differ from a plain program's by a relative error of at most 0.009.
Values may be sent and summed in bfloat16 or wider, within the bound.
No kernel may reach another device: no remote copies, remote signals or barrier semaphores. Data moves between devices by JAX's collectives and lax.ppermute only.
A program may use at most 64 MiB of HBM per device.

v0:
```python
import jax
import jax.numpy as jnp
from jax import lax
from jax.sharding import PartitionSpec as P

D = 8192
BAL = 3


def per_device(hidden, norm_gain, lm_head, loss_count, loss_pos, targets, dest):
    my_rank = lax.axis_index("dp")
    slot_count = loss_pos.shape[1]
    vocab_local = lm_head.shape[0]
    slot_ids = jnp.arange(slot_count, dtype=jnp.int32)
    live_slots = slot_ids < loss_count[0]
    positions = loss_pos[0]
    picked = jnp.take(hidden, positions, axis=0).astype(jnp.float32)
    squares = lax.psum(jnp.sum(picked * picked, axis=1), "tensor")
    inverse = lax.rsqrt(squares / D + 1e-06)
    normed = (picked * norm_gain[None, :] * inverse[:, None]).astype(jnp.bfloat16)
    wanted = jnp.where(live_slots, targets[0], -1)
    placed = jnp.where(live_slots, dest[0], -1)
    all_rows, all_targets, all_places = (
        lax.all_gather(normed, "dp", axis=0, tiled=True),
        lax.all_gather(wanted, "dp", axis=0, tiled=True),
        lax.all_gather(placed, "dp", axis=0, tiled=True),
    )
    partial_logits = lax.dot_general(
        all_rows, lm_head, (((1,), (1,)), ((), ())), preferred_element_type=jnp.float32
    )
    logits = lax.psum(partial_logits, "tensor")
    vocab_start = my_rank * vocab_local
    local_target = all_targets - vocab_start
    columns = jnp.arange(vocab_local, dtype=jnp.int32)
    target_hit = columns[None, :] == local_target[:, None]
    target_part = jnp.sum(jnp.where(target_hit, logits, 0.0), axis=1)
    local_top = jnp.max(logits, axis=1)
    top_all = lax.pmax(local_top, "dp")
    local_total = jnp.sum(jnp.exp(logits - top_all[:, None]), axis=1)
    total_all, target_logit = lax.psum((local_total, target_part), "dp")
    log_total = top_all + jnp.log(total_all)
    losses = log_total - target_logit
    row_valid = (all_targets >= 0)[:, None]
    grad_logits = jnp.where(
        row_valid, jnp.exp(logits - log_total[:, None]) - target_hit.astype(jnp.float32), 0.0
    ).astype(jnp.bfloat16)
    matches = all_places[None, :] == (my_rank * BAL + jnp.arange(BAL, dtype=jnp.int32))[:, None]
    row_loss = jnp.sum(jnp.where(matches, losses[None, :], 0.0), axis=1)
    own_grads = lax.psum_scatter(
        jnp.dot(grad_logits, lm_head, preferred_element_type=jnp.float32),
        "dp",
        scatter_dimension=0,
        tiled=True,
    )
    scaled = own_grads * norm_gain[None, :]
    inner_sum = lax.psum(jnp.sum(scaled * picked, axis=1), "tensor")
    grad_picked = (
        scaled * inverse[:, None] - picked * (inner_sum * inverse * inverse * inverse / D)[:, None]
    )
    grad_rows = jnp.where(live_slots[:, None], grad_picked, 0.0).astype(jnp.bfloat16)
    token_hits = (
        jnp.arange(hidden.shape[0], dtype=jnp.int32)[:, None] == positions[None, :]
    ) & live_slots[None, :]
    hidden_grad = jnp.dot(
        token_hits.astype(jnp.bfloat16), grad_rows, preferred_element_type=jnp.float32
    ).astype(jnp.bfloat16)
    return (hidden_grad, row_loss)


def solution(mesh):
    placed = (
        P("dp", "tensor"),
        P("tensor"),
        P("dp", "tensor"),
        P("dp"),
        P("dp", None),
        P("dp", None),
        P("dp", None),
    )
    return jax.shard_map(
        per_device,
        mesh=mesh,
        in_specs=placed,
        out_specs=(P("dp", "tensor"), P("dp")),
        check_vma=False,
    )
```

profile of v0, /device:TPU:41, one launch (start us, length us, event | category | flops | bytes accessed | tf_op | source)
XLA Modules:
  0.0 764.2 jit_solution(9805195834859717657)
XLA Ops:
  10.6 12.4 %psum.35 = f32[6]{0:T(128)S(1)} all-reduce(f32[6]{0:T(128)S(1)} %fusion.12), channel_id=1, replica_groups=mesh['dp'=64,'tensor'=8] {'tensor'}, use_global_device_ids=true, to_apply=%region_1.2 | all-reduce | flops 6 | bytes 48 | tf_op jit(solution)/shard_map/psum | solution.py:18
  23.8 89.1 %all-gather = bf16[64,6,1024]{2,1,0:T(8,128)(2,1)} all-gather(bf16[1,6,1024]{2,1,0:T(8,128)(2,1)S(1)} %fusion.18), channel_id=1, replica_groups=mesh['dp'=64,'tensor'=8] {'dp'}, dimensions={0}, use_global_device_ids=true | all-gather | bytes 798720 | tf_op jit(solution)/shard_map/all_gather | solution.py:24
  114.4 2.5 fusion.33
  119.0 20.5 %all-reduce.4 = (s32[384]{0:T(512)S(1)}, s32[384]{0:T(512)S(1)}) all-reduce(s32[384]{0:T(512)S(1)} %fusion.27, s32[384]{0:T(512)S(1)} %fusion.26), channel_id=1, replica_groups=mesh['dp'=64,'tensor'=8] {'dp'}, use_global_device_ids=true, to_apply=%add | all-reduce | flops 768 | bytes 6144
  139.5 78.7 %all-reduce.8.cloned.1.call-done = f32[384,1280]{1,0:T(8,128)} async-done(((f32[384,1280]{1,0:T(8,128)}), f32[384,1280]{1,0:T(8,128)}) %all-reduce.8.cloned.1.call-update) | async-done | bytes 1966096 | tf_op jit(solution)/shard_map/psum | solution.py:31
  220.0 92.5 %pmax.7 = f32[384]{0:T(512)S(1)} all-reduce(f32[384]{0:T(512)S(1)} %reduce_max.9), channel_id=1, replica_groups=mesh['dp'=64,'tensor'=8] {'dp'}, use_global_device_ids=true, to_apply=%region_4.5 | all-reduce | flops 384 | bytes 3072 | tf_op jit(solution)/shard_map/pmax | solution.py:38
  312.5 2.3 select_reduce_fusion
  314.8 110.3 %all-reduce.5 = (f32[384]{0:T(512)S(1)}, f32[384]{0:T(512)S(1)}) all-reduce(f32[384]{0:T(512)S(1)} %get-tuple-element.3, f32[384]{0:T(512)S(1)} %get-tuple-element.2), channel_id=1, replica_groups=mesh['dp'=64,'tensor'=8] {'dp'}, use_global_device_ids=true, to_apply=%region_6.7 | all-reduce | flops 768 | bytes 6144 | tf_op jit(solution)/shard_map/psum | solution.py:40
  425.1 4.0 fusion.1
  429.1 123.6 %fusion = f32[8,1024]{1,0:T(8,128)S(1)} fusion(f32[384,1024]{1,0:T(8,128)} %fusion.1), kind=kCustom, calls=%all-reduce-scatter | all-reduce-scatter fusion | flops 524289 | bytes 1607680
  558.5 6.1 collective-permute-start.10
  564.6 21.8 %collective-permute-start.11 = (f32[8,1024]{1,0:T(8,128)S(1)}, f32[8,1024]{1,0:T(8,128)S(1)}, u32[]{:S(2)}, u32[]{:S(2)}) collective-permute-start(f32[8,1024]{1,0:T(8,128)S(1)} %fusion), channel_id=1, source_target_pairs={{0,96},{8,104},{16,112},{24,120},{32,128},{40,136},{48,144},{56,15... | collective-permute-start | bytes 98312
  586.4 4.3 collective-permute-start.12
  590.8 3.8 collective-permute-start.13
  596.5 6.1 collective-permute-start.2
  602.6 5.7 collective-permute-start.3
  610.3 5.5 collective-permute-start.5
  615.9 4.3 collective-permute-start.6
  620.2 4.8 collective-permute-start.7
  625.0 7.4 collective-permute-start.8
  635.5 2.9 collective-permute-done.8
  639.1 4.9 collective-permute-done.9
  644.0 7.1 concatenate
  652.0 103.6 %psum.38 = f32[6]{0:T(128)S(1)} all-reduce(f32[6]{0:T(128)S(1)} %fusion.13), channel_id=1, replica_groups=mesh['dp'=64,'tensor'=8] {'tensor'}, use_global_device_ids=true, to_apply=%region_9.10 | all-reduce | flops 6 | bytes 48 | tf_op jit(solution)/shard_map/psum | solution.py:56
  (72 shorter events, 23.4 us)
Async XLA Ops:
  7.2 107.2 %copy-start = (bf16[1280,1024]{1,0:T(8,128)(2,1)S(1)}, bf16[1280,1024]{1,0:T(8,128)(2,1)}, u32[]{:S(2)}) copy-start(bf16[1280,1024]{1,0:T(8,128)(2,1)} %param.9) | copy-start | bytes 7864324
  7.2 211.1 %all-reduce.8.cloned.1.call-start = ((), (), s32[]{:S(2)}) async-start(), calls=%async_computation | async-start | bytes 3932160 | tf_op jit(solution)/shard_map/psum | solution.py:31
  23.0 91.3 %copy-start.12 = (f32[6]{0:T(128)}, f32[6]{0:T(128)S(1)}, u32[]{:S(2)}) copy-start(f32[6]{0:T(128)S(1)} %psum.35) | copy-start | bytes 76
  429.1 222.0 %copy-start.1 = (f32[1024]{0:T(1024)S(1)}, f32[1024]{0:T(1024)}, u32[]{:S(2)}) copy-start(f32[1024]{0:T(1024)} %param.8) | copy-start | bytes 12292
  429.1 327.1 %copy-start.8 = (s32[1,6]{1,0:T(1,128)S(1)}, s32[1,6]{1,0:T(1,128)}, u32[]{:S(2)}) copy-start(s32[1,6]{1,0:T(1,128)} %param.11) | copy-start | bytes 76
  552.7 33.7 %collective-permute-start.15 = (f32[6,1024]{1,0:T(8,128)S(1)}, f32[6,1024]{1,0:T(8,128)S(1)}, u32[]{:S(2)}, u32[]{:S(2)}) collective-permute-start(f32[6,1024]{1,0:T(8,128)S(1)} %slice.2), channel_id=1, source_target_pairs={{0,128},{8,136},{16,144},{24,152},{32,160},{40,168},{48,176},{56,1... | collective-permute-start | bytes 73736
  554.6 36.2 %collective-permute-start = (f32[8,1024]{1,0:T(8,128)S(1)}, f32[8,1024]{1,0:T(8,128)S(1)}, u32[]{:S(2)}, u32[]{:S(2)}) collective-permute-start(f32[8,1024]{1,0:T(8,128)S(1)} %fusion), channel_id=1, source_target_pairs={{0,8},{8,16},{16,24},{24,32},{32,40},{40,48},{48,56},{56,64},{64,7... | collective-permute-start | bytes 98312
  556.5 38.0 %collective-permute-start.1 = (f32[8,1024]{1,0:T(8,128)S(1)}, f32[8,1024]{1,0:T(8,128)S(1)}, u32[]{:S(2)}, u32[]{:S(2)}) collective-permute-start(f32[8,1024]{1,0:T(8,128)S(1)} %fusion), channel_id=1, source_target_pairs={{0,16},{8,24},{16,32},{24,40},{32,48},{40,56},{48,64},{56,72},{64,... | collective-permute-start | bytes 98312
  558.5 38.1 %collective-permute-start.10 = (f32[8,1024]{1,0:T(8,128)S(1)}, f32[8,1024]{1,0:T(8,128)S(1)}, u32[]{:S(2)}, u32[]{:S(2)}) collective-permute-start(f32[8,1024]{1,0:T(8,128)S(1)} %fusion), channel_id=1, source_target_pairs={{0,88},{8,96},{16,104},{24,112},{32,120},{40,128},{48,136},{56,144... | collective-permute-start | bytes 98312
  564.6 38.0 %collective-permute-start.11 = (f32[8,1024]{1,0:T(8,128)S(1)}, f32[8,1024]{1,0:T(8,128)S(1)}, u32[]{:S(2)}, u32[]{:S(2)}) collective-permute-start(f32[8,1024]{1,0:T(8,128)S(1)} %fusion), channel_id=1, source_target_pairs={{0,96},{8,104},{16,112},{24,120},{32,128},{40,136},{48,144},{56,15... | collective-permute-start | bytes 98312
  586.4 21.9 %collective-permute-start.12 = (f32[8,1024]{1,0:T(8,128)S(1)}, f32[8,1024]{1,0:T(8,128)S(1)}, u32[]{:S(2)}, u32[]{:S(2)}) collective-permute-start(f32[8,1024]{1,0:T(8,128)S(1)} %fusion), channel_id=1, source_target_pairs={{0,104},{8,112},{16,120},{24,128},{32,136},{40,144},{48,152},{56,1... | collective-permute-start | bytes 98312
  590.8 19.5 %collective-permute-start.13 = (f32[8,1024]{1,0:T(8,128)S(1)}, f32[8,1024]{1,0:T(8,128)S(1)}, u32[]{:S(2)}, u32[]{:S(2)}) collective-permute-start(f32[8,1024]{1,0:T(8,128)S(1)} %fusion), channel_id=1, source_target_pairs={{0,112},{8,120},{16,128},{24,136},{32,144},{40,152},{48,160},{56,1... | collective-permute-start | bytes 98312
  594.6 21.3 %collective-permute-start.14 = (f32[8,1024]{1,0:T(8,128)S(1)}, f32[8,1024]{1,0:T(8,128)S(1)}, u32[]{:S(2)}, u32[]{:S(2)}) collective-permute-start(f32[8,1024]{1,0:T(8,128)S(1)} %fusion), channel_id=1, source_target_pairs={{0,120},{8,128},{16,136},{24,144},{32,152},{40,160},{48,168},{56,1... | collective-permute-start | bytes 98312
  596.5 23.6 %collective-permute-start.2 = (f32[8,1024]{1,0:T(8,128)S(1)}, f32[8,1024]{1,0:T(8,128)S(1)}, u32[]{:S(2)}, u32[]{:S(2)}) collective-permute-start(f32[8,1024]{1,0:T(8,128)S(1)} %fusion), channel_id=1, source_target_pairs={{0,24},{8,32},{16,40},{24,48},{32,56},{40,64},{48,72},{56,80},{64,... | collective-permute-start | bytes 98312
  602.6 22.4 %collective-permute-start.3 = (f32[8,1024]{1,0:T(8,128)S(1)}, f32[8,1024]{1,0:T(8,128)S(1)}, u32[]{:S(2)}, u32[]{:S(2)}) collective-permute-start(f32[8,1024]{1,0:T(8,128)S(1)} %fusion), channel_id=1, source_target_pairs={{0,32},{8,40},{16,48},{24,56},{32,64},{40,72},{48,80},{56,88},{64,... | collective-permute-start | bytes 98312
  608.4 24.1 %collective-permute-start.4 = (f32[8,1024]{1,0:T(8,128)S(1)}, f32[8,1024]{1,0:T(8,128)S(1)}, u32[]{:S(2)}, u32[]{:S(2)}) collective-permute-start(f32[8,1024]{1,0:T(8,128)S(1)} %fusion), channel_id=1, source_target_pairs={{0,40},{8,48},{16,56},{24,64},{32,72},{40,80},{48,88},{56,96},{64,... | collective-permute-start | bytes 98312
  610.3 24.7 %collective-permute-start.5 = (f32[8,1024]{1,0:T(8,128)S(1)}, f32[8,1024]{1,0:T(8,128)S(1)}, u32[]{:S(2)}, u32[]{:S(2)}) collective-permute-start(f32[8,1024]{1,0:T(8,128)S(1)} %fusion), channel_id=1, source_target_pairs={{0,48},{8,56},{16,64},{24,72},{32,80},{40,88},{48,96},{56,104},{64... | collective-permute-start | bytes 98312
  615.9 19.2 %collective-permute-start.6 = (f32[8,1024]{1,0:T(8,128)S(1)}, f32[8,1024]{1,0:T(8,128)S(1)}, u32[]{:S(2)}, u32[]{:S(2)}) collective-permute-start(f32[8,1024]{1,0:T(8,128)S(1)} %fusion), channel_id=1, source_target_pairs={{0,56},{8,64},{16,72},{24,80},{32,88},{40,96},{48,104},{56,112},{6... | collective-permute-start | bytes 98312
  620.2 15.3 %collective-permute-start.7 = (f32[8,1024]{1,0:T(8,128)S(1)}, f32[8,1024]{1,0:T(8,128)S(1)}, u32[]{:S(2)}, u32[]{:S(2)}) collective-permute-start(f32[8,1024]{1,0:T(8,128)S(1)} %fusion), channel_id=1, source_target_pairs={{0,64},{8,72},{16,80},{24,88},{32,96},{40,104},{48,112},{56,120},{... | collective-permute-start | bytes 98312
  625.0 13.4 %copy-start.2 = (f32[8,1024]{1,0:T(8,128)}, f32[8,1024]{1,0:T(8,128)S(1)}, u32[]{:S(2)}) copy-start(f32[8,1024]{1,0:T(8,128)S(1)} %collective-permute-done.3) | copy-start | bytes 98308
  625.0 13.4 %collective-permute-start.8 = (f32[8,1024]{1,0:T(8,128)S(1)}, f32[8,1024]{1,0:T(8,128)S(1)}, u32[]{:S(2)}, u32[]{:S(2)}) collective-permute-start(f32[8,1024]{1,0:T(8,128)S(1)} %fusion), channel_id=1, source_target_pairs={{0,72},{8,80},{16,88},{24,96},{32,104},{40,112},{48,120},{56,128},... | collective-permute-start | bytes 98312
  632.5 6.0 copy-start.3
  632.5 11.5 %collective-permute-start.9 = (f32[8,1024]{1,0:T(8,128)S(1)}, f32[8,1024]{1,0:T(8,128)}, u32[]{:S(2)}, u32[]{:S(2)}) collective-permute-start(f32[8,1024]{1,0:T(8,128)S(1)} %fusion), channel_id=1, source_target_pairs={{0,80},{8,88},{16,96},{24,104},{32,112},{40,120},{48,128},{56,136}... | collective-permute-start | bytes 98312
  635.1 3.4 copy-start.4
  (6 other events, 11.7 us)
Sparse Core Ops, SparseCore 0:
  117.0 101.2 all-reduce.7
where the time goes:
time: 766 us; the launch traced here: 764 us
  blocking collectives  552 us (72%)
  waiting for transfers between devices  87 us (11%)
  starting transfers between devices  81.5 us (11%)
  between operations  16.4 us (2%)
  local copies, waits for them, and re-layouts  11.5 us (2%)
  other arithmetic  8.21 us (1%)
    unnamed x2, blocking collectives  144 us
    psum x1, blocking collectives, per_device(): total_all, target_logit = lax.psum((local_total, target_part), 'dp')  110 us
    psum x1, blocking collectives, per_device(): inner_sum = lax.psum(jnp.sum(scaled * picked, axis=1), 'tensor')  104 us
    pmax x1, blocking collectives, per_device(): top_all = lax.pmax(local_top, 'dp')  92.5 us
    all_gather x1, blocking collectives, per_device(): lax.all_gather(normed, 'dp', axis=0, tiled=True)  89.1 us
    unnamed x16, starting transfers between devices  81.4 us
    psum x1, waiting for transfers between devices, per_device(): logits = lax.psum(partial_logits, 'tensor')  78.7 us
  transfers between devices with their start and end apart: 17, of which 4 were waited for; matrix products, arithmetic and copies ran while one was open for 0% of the time, Pallas kernels for 0%

commit v1 on v0

v1 whole, which is shorter than its diff:
```python
import functools

import jax
import jax.numpy as jnp
from jax import lax
from jax.experimental import pallas as pl
from jax.experimental.pallas import tpu as pltpu
from jax.sharding import Mesh, PartitionSpec as P

D = 8192
BAL = 3
CAP = 6
NY, NZ, NX, NC = 4, 16, 4, 2
N_DP = NY * NZ
N_TENSOR = NX * NC
ROWS = N_DP * BAL
SUB = ROWS // N_TENSOR
SLOT = 8
LANES = 128
STAT_ROW, OWN_ROW = 6, 7
N_STAT = 5
N_PIECE = 3 * N_STAT

VMEM = pl.BlockSpec(memory_space=pltpu.VMEM)
SMEM = pl.BlockSpec(memory_space=pltpu.SMEM)
HBM = pl.BlockSpec(memory_space=pltpu.HBM)
PARAMS = pltpu.CompilerParams(vmem_limit_bytes=24 * 1024 * 1024)
SMALL = pltpu.CompilerParams(vmem_limit_bytes=4 * 1024 * 1024)
f32, bf16, i32 = jnp.float32, jnp.bfloat16, jnp.int32


def dot(a, b, dims):
    return lax.dot_general(a, b, (dims, ((), ())), preferred_element_type=f32)


def pieces(x):
    hi = x.astype(bf16)
    rest = x - hi.astype(f32)
    mid = rest.astype(bf16)
    low = (rest - mid.astype(f32)).astype(bf16)
    return hi.astype(f32), mid.astype(f32), low.astype(f32)


def pick_kernel(hidden, count_in, pos_in, targets_in, dest_in, out, copies_out, count, pos, targets, dest, rows, sems):
    scalars = []
    for k, (src, dst) in enumerate(((pos_in, pos), (count_in, count), (targets_in, targets), (dest_in, dest))):
        scalars.append(pltpu.make_async_copy(src, dst, sems.at[CAP + k]))
        scalars[-1].start()
    scalars[0].wait()
    copies = []
    for s in range(CAP):
        start = pl.multiple_of(jnp.clip(pos[0, s], 0, 255) // 16 * 16, 16)
        copies.append(pltpu.make_async_copy(hidden.at[pl.ds(start, 16), :], rows.at[s], sems.at[s]))
        copies[-1].start()
    for copy in scalars[1:]:
        copy.wait()
    lane = lax.broadcasted_iota(i32, (1, LANES), 1)
    meta = jnp.zeros((1, LANES), f32)
    for s in range(CAP):
        live = s < count[0]
        t = targets[0, s]
        place = jnp.where(live, dest[0, s], -1)
        digits = (t // 65536, t // 256 % 256, t % 256, place)
        for k, digit in enumerate(digits):
            meta = jnp.where(lane == k * SLOT + s, digit.astype(f32), meta)
    sub8 = lax.broadcasted_iota(i32, (SLOT, 1), 0)
    sub16 = lax.broadcasted_iota(i32, (16, 1), 0)
    total = jnp.where(
        sub8 == STAT_ROW,
        jnp.concatenate([meta, jnp.zeros((1, out.shape[1] - LANES), f32)], axis=1),
        0.0,
    )
    for s in range(CAP):
        copies[s].wait()
        one = jnp.where(sub16 == jnp.clip(pos[0, s], 0, 255) % 16, rows[s].astype(f32), 0.0)
        row = jnp.sum(one, axis=0, keepdims=True)
        total = jnp.where(sub8 == s, row, total)
    out[...] = total.astype(bf16)
    copies_out[...] = jnp.concatenate([total] * NZ, axis=0).astype(bf16)


def column(rows8, k):
    lane = lax.broadcasted_iota(i32, (1, SLOT, LANES), 2)
    sub = lax.broadcasted_iota(i32, (1, SLOT, LANES), 1)
    return jnp.sum(jnp.where(lane == k * SLOT + sub, rows8, 0.0), axis=2, keepdims=True)


def logits_kernel(x0, x1, x2, x3, gain, head_in, part, want, spread, head, sem):
    load = pltpu.make_async_copy(head_in, head, sem)
    load.start()
    y = lax.axis_index("y")
    lane = lax.broadcasted_iota(i32, (1, LANES), 1)
    row_lane = lax.broadcasted_iota(i32, (1, ROWS), 1).astype(f32)
    sub = lax.broadcasted_iota(i32, (NZ, SLOT, 1), 1)
    count = NZ * SLOT
    rows = jnp.zeros((ROWS, gain.shape[1]), f32)
    digits = jnp.zeros((ROWS, LANES), f32)
    dests = []
    for x in (x0, x1, x2, x3):
        meta = x[:, :LANES].astype(f32).reshape(NZ, SLOT, LANES)
        meta = jnp.broadcast_to(meta[:, STAT_ROW : STAT_ROW + 1, :], meta.shape)
        dests.append(jnp.where(sub < CAP, column(meta, 3), -1.0).reshape(count, 1))
        hot = (dests[-1] == row_lane).astype(f32).astype(bf16)
        digit = jnp.zeros((count, LANES), f32)
        for k in range(3):
            digit = jnp.where(lane == k, column(meta, k).reshape(count, 1), digit)
        rows = rows + dot(hot, x[...], ((0,), (0,)))
        digits = digits + dot(hot, digit.astype(bf16), ((0,), (0,)))
    target = digits[:, 0:1] * 65536.0 + digits[:, 1:2] * 256.0 + digits[:, 2:3]
    want[...] = jnp.broadcast_to(target, want.shape)
    for other in range(NY):
        dest = dests[0]
        for k in range(1, NY):
            dest = jnp.where((y + k) % NY == other, dests[k], dest)
        spread[other * count : (other + 1) * count, :] = (dest == row_lane).astype(f32).astype(bf16)
    scaled = (rows * gain[...]).astype(bf16)
    vocab = head.shape[0]
    load.wait()
    part[:, :vocab] = dot(scaled, head[...], ((1,), (1,)))
    part[:, vocab:] = jnp.broadcast_to(
        jnp.sum(rows * rows, axis=1, keepdims=True), (ROWS, LANES)
    )


def vocab_ids(vocab):
    start = (lax.axis_index("y") * NZ + lax.axis_index("z")) * vocab
    return (lax.broadcasted_iota(i32, (1, vocab), 1) + start).astype(f32)


def target_kernel(vocab, head, want, spread, out):
    hit = (vocab_ids(vocab) == want[:, 0:1]).astype(f32).astype(bf16)
    hits = dot(hit, head[...], ((1,), (0,))).astype(bf16)
    rows = dot(spread[...], hits, ((1,), (0,))).reshape(NY, NZ, SLOT, head.shape[1])
    for z in range(NZ):
        block = jnp.concatenate([rows[y, z] for y in range(NY)], axis=0)
        out[z * NY * SLOT : (z + 1) * NY * SLOT, :] = block.astype(bf16)


def softmax_kernel(vocab, parts, want, out):
    total = parts[0:SUB, :]
    for t in range(1, N_TENSOR):
        total = total + parts[t * SUB : (t + 1) * SUB, :]
    inverse = lax.rsqrt(total[:, vocab : vocab + 1] / D + 1e-6)
    logits = total[:, :vocab] * inverse
    rank = lax.axis_index("x") * NC + lax.axis_index("core")
    target = want[pl.ds(pl.multiple_of(rank * SUB, SUB), SUB), :][:, 0:1]
    ids = vocab_ids(vocab)
    top = jnp.max(logits, axis=1, keepdims=True)
    down = logits - top
    weight = jnp.exp(down)
    total_w = jnp.sum(weight, axis=1, keepdims=True)
    total_u = jnp.sum(weight * down, axis=1, keepdims=True)
    hit = jnp.sum(jnp.where(ids == target, logits, 0.0), axis=1, keepdims=True)
    lane = lax.broadcasted_iota(i32, (1, LANES), 1)
    stats = jnp.zeros((SUB, LANES), f32)
    for q, value in enumerate((top, total_w, total_u, hit, inverse)):
        for j, piece in enumerate(pieces(value)):
            stats = jnp.where(lane == 3 * q + j, piece, stats)
    out[:, :vocab] = weight.astype(bf16)
    out[:, vocab:] = stats.astype(bf16)


def as_row(columns):
    lane = lax.broadcasted_iota(i32, (1, SLOT, LANES), 2)
    sub = lax.broadcasted_iota(i32, (1, SLOT, LANES), 1)
    total = jnp.zeros(columns.shape, f32)
    for k in range(N_PIECE):
        total = jnp.where(lane == k * SLOT + sub, columns[:, :, k : k + 1], total)
    return jnp.sum(total, axis=1, keepdims=True)


def grad_kernel(vocab, weights, head, spread, out):
    width = head.shape[1]
    grads = dot(weights[:, :vocab], head[...], ((1,), (0,))).astype(bf16)
    stats = weights[:, vocab:]
    hot = spread[...]
    own = lax.broadcasted_iota(i32, (N_DP * SLOT, 1), 0)
    own = jnp.where(own % SLOT < BAL, own // SLOT * BAL + own % SLOT, -1)
    own_hot = (own == lax.broadcasted_iota(i32, (1, ROWS), 1)).astype(f32).astype(bf16)
    slot_stats = dot(hot, stats, ((1,), (0,))).reshape(N_DP, SLOT, LANES)
    own_stats = dot(own_hot, stats, ((1,), (0,))).reshape(N_DP, SLOT, LANES)
    sub = lax.broadcasted_iota(i32, (1, SLOT, 1), 1)
    slot_grads = dot(hot, grads, ((1,), (0,)))
    first = slot_grads[:, :LANES].reshape(N_DP, SLOT, LANES)
    first = jnp.where(sub == STAT_ROW, as_row(slot_stats), first)
    first = jnp.where(sub == OWN_ROW, as_row(own_stats), first)
    out[:, :LANES] = first.reshape(N_DP * SLOT, LANES).astype(bf16)
    out[:, LANES:] = slot_grads[:, LANES:].astype(bf16)


def read_stats(rows, at):
    rows = jnp.broadcast_to(rows[:, at : at + 1, :], rows.shape)
    out = []
    for q in range(N_STAT):
        out.append(column(rows, 3 * q) + column(rows, 3 * q + 1) + column(rows, 3 * q + 2))
    return out


def merge_stats(stats):
    top = functools.reduce(jnp.maximum, [st[0] for st in stats])
    factors = [jnp.exp(st[0] - top) for st in stats]
    total = sum(f * st[1] for f, st in zip(factors, stats))
    total_u = sum(f * (st[2] + st[1] * (st[0] - top)) for f, st in zip(factors, stats))
    hit = sum(st[3] for st in stats)
    return factors, (top, total, total_u, hit, stats[0][4])


def stats_row(stats):
    lane = lax.broadcasted_iota(i32, (1, 1, LANES), 2)
    columns = jnp.zeros(stats[0].shape[:2] + (LANES,), f32)
    for q, value in enumerate(stats):
        for j, piece in enumerate(pieces(value)):
            columns = jnp.where(lane == 3 * q + j, piece, columns)
    return as_row(columns)


def merge_kernel(parts, out):
    width = parts.shape[1]
    size = parts.shape[0] // NY
    blocks = size // SLOT
    slot_stats, own_stats = [], []
    for r in range(NY):
        heads = parts[r * size : (r + 1) * size, :LANES].astype(f32).reshape(blocks, SLOT, LANES)
        slot_stats.append(read_stats(heads, STAT_ROW))
        own_stats.append(read_stats(heads, OWN_ROW))
    factors, merged = merge_stats(slot_stats)
    _, own_merged = merge_stats(own_stats)
    row, own_row = stats_row(merged), stats_row(own_merged)
    sub = lax.broadcasted_iota(i32, (1, SLOT, 1), 1)
    factors = [factor.reshape(size, 1) for factor in factors]
    for c in range(0, width, LANES):
        grads = jnp.zeros((size, LANES), f32)
        for r in range(NY):
            grads = grads + factors[r] * parts[r * size : (r + 1) * size, c : c + LANES].astype(f32)
        if c == 0:
            grads = grads.reshape(blocks, SLOT, LANES)
            grads = jnp.where(sub == STAT_ROW, row, grads)
            grads = jnp.where(sub == OWN_ROW, own_row, grads).reshape(size, LANES)
        out[:, c : c + LANES] = grads.astype(bf16)


def final_kernel(parts, hits, gain, picked, count, pos, out, loss):
    width = parts.shape[1]
    heads = parts[:, :LANES].astype(f32).reshape(NZ, SLOT, LANES)
    slot_all = read_stats(heads, STAT_ROW)
    own_all = read_stats(heads, OWN_ROW)
    factors, (top, total, total_u, hit, inverse) = merge_stats(
        [[value[z : z + 1] for value in slot_all] for z in range(NZ)]
    )
    _, own = merge_stats([[value[z : z + 1] for value in own_all] for z in range(NZ)])
    sub = lax.broadcasted_iota(i32, (SLOT, 1), 0)
    live = sub < count[0]
    safe = jnp.where(live, total[0], 1.0)
    inner = (total_u[0] / safe + top[0] - hit[0]) * inverse[0] * inverse[0] / D
    losses = own[0][0] + jnp.log(jnp.where(sub < BAL, own[1][0], 1.0)) - own[3][0]
    for i in range(BAL):
        loss[i] = jnp.sum(jnp.where(sub == i, losses, 0.0))
    token = lax.broadcasted_iota(i32, (out.shape[0], 1), 0)
    lane = lax.broadcasted_iota(i32, (1, SLOT), 1)
    hot = jnp.zeros((out.shape[0], SLOT), jnp.bool_)
    for s in range(CAP):
        hot = hot | ((lane == s) & (token == pos[0, s]) & (s < count[0]))
    hot = hot.astype(f32).astype(bf16)
    grads = jnp.zeros((SLOT, width), f32)
    pieces_z = parts[...].astype(f32).reshape(NZ, SLOT, width)
    for z in range(NZ):
        grads = grads + factors[z][0] * pieces_z[z]
    hit_rows = jnp.sum(hits[...].astype(f32).reshape(NY, SLOT, width), axis=0)
    grads = (grads / safe - hit_rows) * gain[...]
    rows = grads * inverse[0] - picked[...].astype(f32) * inner
    rows = jnp.where(live, rows, 0.0).astype(bf16)
    out[...] = dot(hot, rows, ((1,), (0,))).astype(bf16)


def per_device(hidden, norm_gain, lm_head, loss_count, loss_pos, targets, dest):
    vocab, width = lm_head.shape
    tokens = hidden.shape[0]
    gain = norm_gain.reshape(1, width)
    shape = jax.ShapeDtypeStruct
    picked, copies = pl.pallas_call(
        pick_kernel,
        out_shape=(shape((SLOT, width), bf16), shape((NZ * SLOT, width), bf16)),
        in_specs=[HBM] * 5,
        out_specs=(VMEM, VMEM),
        scratch_shapes=[
            pltpu.SMEM((1,), i32),
            pltpu.SMEM((1, CAP), i32),
            pltpu.SMEM((1, CAP), i32),
            pltpu.SMEM((1, CAP), i32),
            pltpu.VMEM((CAP, 16, width), bf16),
            pltpu.SemaphoreType.DMA((CAP + 4,)),
        ],
        compiler_params=SMALL,
        name="pick_rows",
    )(hidden, loss_count, loss_pos, targets, dest)
    rows = lax.all_to_all(copies, "z", 0, 0, tiled=True)
    others = [lax.ppermute(rows, "y", [((i + k) % NY, i) for i in range(NY)]) for k in range(1, NY)]
    part, want, spread = pl.pallas_call(
        logits_kernel,
        out_shape=(
            shape((ROWS, vocab + LANES), f32),
            shape((ROWS, LANES), f32),
            shape((N_DP * SLOT, ROWS), bf16),
        ),
        in_specs=[VMEM] * 5 + [HBM],
        out_specs=(VMEM, VMEM, VMEM),
        scratch_shapes=[pltpu.VMEM((vocab, width), bf16), pltpu.SemaphoreType.DMA(())],
        compiler_params=PARAMS,
        name="partial_logits",
    )(rows, *others, gain, lm_head)
    hits = pl.pallas_call(
        functools.partial(target_kernel, vocab),
        out_shape=shape((N_DP * SLOT, width), bf16),
        in_specs=[VMEM] * 3,
        out_specs=VMEM,
        compiler_params=PARAMS,
        name="target_rows",
    )(lm_head, want, spread)
    hits = lax.psum_scatter(hits, "z", scatter_dimension=0, tiled=True)
    hits = lax.all_to_all(hits, "y", 0, 0, tiled=True)
    parts = lax.all_to_all(part, ("x", "core"), 0, 0, tiled=True)
    weights = pl.pallas_call(
        functools.partial(softmax_kernel, vocab),
        out_shape=shape((SUB, vocab + LANES), bf16),
        in_specs=[VMEM] * 2,
        out_specs=VMEM,
        compiler_params=PARAMS,
        name="local_softmax",
    )(parts, want)
    weights = lax.all_gather(weights, ("x", "core"), axis=0, tiled=True)
    blocks = pl.pallas_call(
        functools.partial(grad_kernel, vocab),
        out_shape=shape((N_DP * SLOT, width), bf16),
        in_specs=[VMEM] * 3,
        out_specs=VMEM,
        compiler_params=PARAMS,
        name="partial_grads",
    )(weights, lm_head, spread)
    blocks = lax.all_to_all(blocks, "y", 0, 0, tiled=True)
    blocks = pl.pallas_call(
        merge_kernel,
        out_shape=shape((NZ * SLOT, width), bf16),
        in_specs=[VMEM],
        out_specs=VMEM,
        compiler_params=PARAMS,
        name="merge_y",
    )(blocks)
    blocks = lax.all_to_all(blocks, "z", 0, 0, tiled=True)
    hidden_grad, row_loss = pl.pallas_call(
        final_kernel,
        out_shape=(shape((tokens, width), bf16), shape((BAL,), f32)),
        in_specs=[VMEM, VMEM, VMEM, VMEM, SMEM, SMEM],
        out_specs=(VMEM, SMEM),
        compiler_params=PARAMS,
        name="merge_z",
    )(blocks, hits, gain, picked, loss_count, loss_pos)
    return hidden_grad, row_loss


def solution(mesh):
    wide = Mesh(mesh.devices.reshape(NY, NZ, NX, NC), ("y", "z", "x", "core"))
    dp, tensor = ("y", "z"), ("x", "core")
    return jax.shard_map(
        per_device,
        mesh=wide,
        in_specs=(
            P(dp, tensor),
            P(tensor),
            P(dp, tensor),
            P(dp),
            P(dp, None),
            P(dp, None),
            P(dp, None),
        ),
        out_specs=(P(dp, tensor), P(dp)),
        check_vma=False,
    )
```

time: 766 us -> 181 us (0.24)
  the two profiles are of different devices: /device:TPU:41 before, /device:TPU:34 now
where the time goes in v1:
time: 181 us; the launch traced here: 180 us
  blocking collectives  109 us (60%)
  waiting for transfers between devices  20.1 us (11%)
  starting transfers between devices  16 us (9%)
  between operations  14.8 us (8%)
  Pallas kernels  12.7 us (7%)
  local copies, waits for them, and re-layouts  7.4 us (4%)
    all_to_all x1, blocking collectives, per_device(): rows = lax.all_to_all(copies, 'z', 0, 0, tiled=True)  32.9 us
    all_to_all x1, blocking collectives, per_device(): blocks = lax.all_to_all(blocks, 'z', 0, 0, tiled=True)  24.1 us
    all_to_all x1, blocking collectives, per_device(): parts = lax.all_to_all(part, ('x', 'core'), 0, 0, tiled=True)  19.8 us
    all_to_all x1, blocking collectives, per_device(): blocks = lax.all_to_all(blocks, 'y', 0, 0, tiled=True)  19.8 us
    all_gather x1, blocking collectives, per_device(): weights = lax.all_gather(weights, ('x', 'core'), axis=0, tiled=True)  12.5 us
    ppermute x3, starting transfers between devices, per_device(): lax.ppermute(rows, 'y', [((i + k) % NY, i) for i in range(NY)])  11.5 us
    reduce_scatter x1, waiting for transfers between devices, per_device(): hits = lax.psum_scatter(hits, 'z', scatter_dimension=0, tiled=True)  10 us
    unnamed x22, local copies, waits for them, and re-layouts  7.4 us
  transfers between devices with their start and end apart: 5, of which 4 were waited for; matrix products, arithmetic and copies ran while one was open for 0% of the time, Pallas kernels for 3%

profile of v1, /device:TPU:34, one launch (start us, length us, event | category | flops | bytes accessed | tf_op | source)
XLA Modules:
  0.0 180.3 jit_solution(3156438929158268566)
XLA Ops:
  7.9 1.0 copy-done.4
  10.9 1.2 pick_rows.1
  12.1 32.9 %all_to_all.55 = bf16[16,8,1024]{2,1,0:T(8,128)(2,1)S(1)} all-to-all(bf16[16,8,1024]{2,1,0:T(8,128)(2,1)S(1)} %bitcast.21), channel_id=1, replica_groups=mesh['y'=4,'z'=16,'x'=4,'core'=2] {'z'}, dimensions={0} | all-to-all | bytes 524288 | tf_op jit(solution)/shard_map/all_to_all | solution.py:296
  45.0 3.5 %collective-permute-start.2 = (bf16[128,1024]{1,0:T(8,128)(2,1)S(1)}, bf16[128,1024]{1,0:T(8,128)(2,1)S(1)}, u32[]{:S(2)}, u32[]{:S(2)}) collective-permute-start(bf16[128,1024]{1,0:T(8,128)(2,1)S(1)} %bitcast.15), channel_id=1, source_target_pairs={{384,0},{0,128},{128,256},{256,384},{385,1},{1,129},{129,257},{257... | collective-permute-start | bytes 786440 | tf_op jit(solution)/shard_map/ppermute | solution.py:297
  48.5 4.8 %collective-permute-start.1 = (bf16[128,1024]{1,0:T(8,128)(2,1)S(1)}, bf16[128,1024]{1,0:T(8,128)(2,1)S(1)}, u32[]{:S(2)}, u32[]{:S(2)}) collective-permute-start(bf16[128,1024]{1,0:T(8,128)(2,1)S(1)} %bitcast.16), channel_id=1, source_target_pairs={{256,0},{384,128},{0,256},{128,384},{257,1},{385,129},{1,257},{129... | collective-permute-start | bytes 786440 | tf_op jit(solution)/shard_map/ppermute | solution.py:297
  53.3 3.3 %collective-permute-start = (bf16[128,1024]{1,0:T(8,128)(2,1)S(1)}, bf16[128,1024]{1,0:T(8,128)(2,1)S(1)}, u32[]{:S(2)}, u32[]{:S(2)}) collective-permute-start(bf16[128,1024]{1,0:T(8,128)(2,1)S(1)} %bitcast.17), channel_id=1, source_target_pairs={{128,0},{256,128},{384,256},{0,384},{129,1},{257,129},{385,257},{1... | collective-permute-start | bytes 786440 | tf_op jit(solution)/shard_map/ppermute | solution.py:297
  56.6 5.6 %collective-permute-done.1.x2 = bf16[128,1024]{1,0:T(8,128)(2,1)S(1)} collective-permute-done((bf16[128,1024]{1,0:T(8,128)(2,1)S(1)}, bf16[128,1024]{1,0:T(8,128)(2,1)S(1)}, u32[]{:S(2)}, u32[]{:S(2)}) %collective-permute-start.1) | collective-permute-done | bytes 262176 | tf_op jit(solution)/shard_map/ppermute | solution.py:297
  62.2 1.3 collective-permute-done.x1
  63.5 1.7 copy-done
  65.2 0.7 copy-done.5
  65.9 2.4 %partial_logits.1 = (f32[192,1408]{1,0:T(8,128)S(1)}, f32[192,128]{1,0:T(8,128)S(1)}, bf16[512,192]{1,0:T(8,128)(2,1)S(1)}) custom-call(bf16[128,1024]{1,0:T(8,128)(2,1)S(1)} %bitcast.18, bf16[128,1024]{1,0:T(8,128)(2,1)S(1)} %collective-permute-done.x1, bf16[128,1024]{1,0:T(8,128)(2,1)S(1)} %collective-permute-done.1.x2, ...), custom_call_target="tpu_custom_call" | custom-call | tf_op jit(solution)/shard_map/partial_logits/pallas_call | solution.py:298
  68.3 1.0 copy-done.3
  69.3 1.0 target_rows.1
  70.3 1.0 copy-done.2
  71.3 19.8 %all_to_all.56 = f32[8,24,1408]{2,1,0:T(8,128)S(1)} all-to-all(f32[8,24,1408]{2,1,0:T(8,128)} %bitcast.14), channel_id=1, replica_groups=mesh['y'=4,'z'=16,'x'=4,'core'=2] {'x','core'}, dimensions={0} | all-to-all | bytes 2162688 | tf_op jit(solution)/shard_map/all_to_all | solution.py:321
  91.5 12.5 %all_gather.3.weights = bf16[192,1408]{1,0:T(8,128)(2,1)S(1)} all-gather(bf16[24,1408]{1,0:T(8,128)(2,1)S(1)} %local_softmax.1), channel_id=1, replica_groups=mesh['y'=4,'z'=16,'x'=4,'core'=2] {'x','core'}, dimensions={0}, use_global_device_ids=true | all-gather | bytes 608256 | tf_op jit(solution)/shard_map/all_gather | solution.py:330
  104.0 3.2 %partial_grads.1 = bf16[512,1024]{1,0:T(8,128)(2,1)S(1)} custom-call(bf16[192,1408]{1,0:T(8,128)(2,1)S(1)} %all_gather.3.weights, bf16[1280,1024]{1,0:T(8,128)(2,1)S(1)} %copy-done.1, bf16[512,192]{1,0:T(8,128)(2,1)S(1)} %get-tuple-element.10.spread), custom_call_target="tpu_custom_call" | custom-call | tf_op jit(solution)/shard_map/partial_grads/pallas_call | solution.py:331
  107.2 19.8 %all_to_all.57 = bf16[4,128,1024]{2,1,0:T(8,128)(2,1)S(1)} all-to-all(bf16[4,128,1024]{2,1,0:T(8,128)(2,1)S(1)} %bitcast.12), channel_id=1, replica_groups=mesh['y'=4,'z'=16,'x'=4,'core'=2] {'y'}, dimensions={0} | all-to-all | bytes 2097152 | tf_op jit(solution)/shard_map/all_to_all | solution.py:339
  127.0 10.0 %reduce-scatter.2.cloned.1.call-done = bf16[32,1024]{1,0:T(8,128)(2,1)} async-done(((bf16[512,1024]{1,0:T(8,128)(2,1)}), bf16[32,1024]{1,0:T(8,128)(2,1)}) %reduce-scatter.2.cloned.1.call-update) | async-done | bytes 65552 | tf_op jit(solution)/shard_map/reduce_scatter | solution.py:319
  137.1 4.4 %all-to-all-start.4 = ((bf16[4,8,1024]{2,1,0:T(8,128)(2,1)}), bf16[4,8,1024]{2,1,0:T(8,128)(2,1)S(1)}, u32[]{:S(2)}, u32[]{:S(2)}) async-start(bf16[4,8,1024]{2,1,0:T(8,128)(2,1)} %bitcast.25), calls=%async_computation.5 | async-start | bytes 131072 | tf_op jit(solution)/shard_map/all_to_all | solution.py:320
  141.5 2.5 %merge_y.1 = bf16[128,1024]{1,0:T(8,128)(2,1)S(1)} custom-call(bf16[512,1024]{1,0:T(8,128)(2,1)S(1)} %bitcast.13), custom_call_target="tpu_custom_call" | custom-call | tf_op jit(solution)/shard_map/merge_y/pallas_call | solution.py:340
  144.0 3.1 %all-to-all-done.4 = bf16[4,8,1024]{2,1,0:T(8,128)(2,1)S(1)} async-done(((bf16[4,8,1024]{2,1,0:T(8,128)(2,1)}), bf16[4,8,1024]{2,1,0:T(8,128)(2,1)S(1)}, u32[]{:S(2)}, u32[]{:S(2)}) %all-to-all-start.4) | async-done | bytes 65568 | tf_op jit(solution)/shard_map/all_to_all | solution.py:320
  147.1 24.1 %all_to_all.58 = bf16[16,8,1024]{2,1,0:T(8,128)(2,1)S(1)} all-to-all(bf16[16,8,1024]{2,1,0:T(8,128)(2,1)S(1)} %bitcast.19), channel_id=1, replica_groups=mesh['y'=4,'z'=16,'x'=4,'core'=2] {'z'}, dimensions={0} | all-to-all | bytes 524288 | tf_op jit(solution)/shard_map/all_to_all | solution.py:348
  171.3 2.2 %merge_z.1 = (bf16[256,1024]{1,0:T(8,128)(2,1)}, f32[3]{0:T(128)}) custom-call(bf16[128,1024]{1,0:T(8,128)(2,1)S(1)} %bitcast.20, bf16[32,1024]{1,0:T(8,128)(2,1)S(1)} %bitcast.22, f32[1,1024]{1,0:T(1,128)S(1)} %bitcast.24, bf16[8,1024]{1,0:T(8,128)(2,1)S(1)} %get-tuple-element.11.picked, s32[1]{0:T(128)S(6)} %copy.9.count_in.count, s32[1,6]{1,0:T(1,128)S(1)} %copy-done.8), custom_call_target="tpu_custom_call" | custom-call | tf_op jit(solution)/shard_map/merge_z/pallas_call | solution.py:349
  (21 shorter events, 2.3 us)
Async XLA Ops:
  7.2 129.9 %reduce-scatter.2.cloned.1.call-start = ((), (), s32[]{:S(2)}) async-start(), calls=%async_computation.6 | async-start | bytes 1114112 | tf_op jit(solution)/shard_map/reduce_scatter | solution.py:319
  7.9 1.0 copy-start.4
  8.9 0.7 copy-start.7
  9.6 0.7 copy-start.9
  10.2 0.7 copy-start.10
  45.0 11.6 %collective-permute-start.2 = (bf16[128,1024]{1,0:T(8,128)(2,1)S(1)}, bf16[128,1024]{1,0:T(8,128)(2,1)S(1)}, u32[]{:S(2)}, u32[]{:S(2)}) collective-permute-start(bf16[128,1024]{1,0:T(8,128)(2,1)S(1)} %bitcast.15), channel_id=1, source_target_pairs={{384,0},{0,128},{128,256},{256,384},{385,1},{1,129},{129,257},{257... | collective-permute-start | bytes 786440 | tf_op jit(solution)/shard_map/ppermute | solution.py:297
  48.5 13.7 %collective-permute-start.1 = (bf16[128,1024]{1,0:T(8,128)(2,1)S(1)}, bf16[128,1024]{1,0:T(8,128)(2,1)S(1)}, u32[]{:S(2)}, u32[]{:S(2)}) collective-permute-start(bf16[128,1024]{1,0:T(8,128)(2,1)S(1)} %bitcast.16), channel_id=1, source_target_pairs={{256,0},{384,128},{0,256},{128,384},{257,1},{385,129},{1,257},{129... | collective-permute-start | bytes 786440 | tf_op jit(solution)/shard_map/ppermute | solution.py:297
  53.3 10.2 %collective-permute-start = (bf16[128,1024]{1,0:T(8,128)(2,1)S(1)}, bf16[128,1024]{1,0:T(8,128)(2,1)S(1)}, u32[]{:S(2)}, u32[]{:S(2)}) collective-permute-start(bf16[128,1024]{1,0:T(8,128)(2,1)S(1)} %bitcast.17), channel_id=1, source_target_pairs={{128,0},{256,128},{384,256},{0,384},{129,1},{257,129},{385,257},{1... | collective-permute-start | bytes 786440 | tf_op jit(solution)/shard_map/ppermute | solution.py:297
  63.5 1.7 copy-start
  65.2 0.7 copy-start.5
  65.9 3.4 %copy-start.1 = (bf16[1280,1024]{1,0:T(8,128)(2,1)S(1)}, bf16[1280,1024]{1,0:T(8,128)(2,1)}, u32[]{:S(2)}) copy-start(bf16[1280,1024]{1,0:T(8,128)(2,1)} %head.3) | copy-start | bytes 7864324
  68.3 1.0 copy-start.3
  70.3 1.0 copy-start.2
  127.0 44.2 %copy-start.6 = (f32[1024]{0:T(1024)S(1)}, f32[1024]{0:T(1024)}, u32[]{:S(2)}) copy-start(f32[1024]{0:T(1024)} %param.8) | copy-start | bytes 12292
  127.0 44.2 %copy-start.8 = (s32[1,6]{1,0:T(1,128)S(1)}, s32[1,6]{1,0:T(1,128)}, u32[]{:S(2)}) copy-start(s32[1,6]{1,0:T(1,128)} %pos.1) | copy-start | bytes 76
  137.1 10.1 %all-to-all-start.4 = ((bf16[4,8,1024]{2,1,0:T(8,128)(2,1)}), bf16[4,8,1024]{2,1,0:T(8,128)(2,1)S(1)}, u32[]{:S(2)}, u32[]{:S(2)}) async-start(bf16[4,8,1024]{2,1,0:T(8,128)(2,1)} %bitcast.25), calls=%async_computation.5 | async-start | bytes 131072 | tf_op jit(solution)/shard_map/all_to_all | solution.py:320
Sparse Core Ops, SparseCore 0:
  71.4 65.5 reduce-scatter.1
